TPU v7x, 128 devices: a whole 4x4x4 slice. The times are simulated.
128 devices in a mesh: grp: 4 (over x_hi, core), tile: 32 (over x_lo, y, z).
Axes of the slice: x: 4 (x_hi: 2, x_lo: 2; x = x_hi * 2 + x_lo), y: 4, z: 4, core: 2. Of those that a mesh axis runs over, the one named last changes fastest.
Arguments:
- start_field: float32 [512, 512, 512], P('grp', 'tile'), may hold values from -4 to 4
- class_ids: int32 [512, 512], P('tile'), may hold values from 0 to 7
- run_levels: int32 [512, 8], replicated, may hold values from 0 to 7
- steepness: float32 [512], replicated, may hold values from 0.1 to 1
- step_pick: int32 [512], replicated, may hold values from 1 to 4
- input_layer: float32 [69, 2048], replicated, may hold values from -2 to 2
- output_layer: bfloat16 [2048, 262144], P(None, ('grp', 'tile')), may hold values from -0.125 to 0.125
- output_bias: float32 [262144], P(('grp', 'tile')), may hold values from -1.5 to 1.5
Outputs:
- misfit: bfloat16 [512, 262144], P(None, ('grp', 'tile'))
- output_next: bfloat16 [2048, 262144], P(None, ('grp', 'tile'))
- bias_next: float32 [262144], P(('grp', 'tile'))
- input_next: float32 [69, 2048], replicated
All inputs are finite; a program needn't handle non-finite values.
Results may differ from a plain program's by a relative error of at most 0.0029.
The roundings to bfloat16 on the way count: a program that leaves them out, or rounds other values in their place, can miss the bound.
Values sent between devices are 32-bit elements; how exact they have to be, the bound alone decides.
A program may use at most 128 MiB of HBM per device.

v0:
```python
import jax
import jax.numpy as jnp
from jax import lax
from jax.sharding import Mesh
from jax.sharding import PartitionSpec as P

STEPS = 4
LEVELS = 8
GRP = ("grp_0", "grp_1")
GRP_TILE = ("grp_0", "grp_1", "tile")


def with_halo(value, sides, width):
    for axis, dim in sides:
        size, length = (lax.axis_size(axis), value.shape[dim])
        up = [(i, (i + 1) % size) for i in range(size - 1)]
        down = [(j, i) for i, j in up]
        last = lax.slice_in_dim(value, length - width, length, axis=dim)
        initial = lax.slice_in_dim(value, 0, width, axis=dim)
        before = lax.ppermute(last, axis, up)
        after = lax.ppermute(initial, axis, down)
        value = jnp.concatenate([before, value, after], axis=dim)
    return value


def in_blocks(value, dim, length):
    shape = value.shape
    tiles = value.reshape(*shape[:dim], length, shape[dim] // length, *shape[dim + 1 :])
    return jnp.moveaxis(tiles, dim, 0)


def in_order(tiles, dim):
    tiles = jnp.moveaxis(tiles, 0, dim)
    shape = tiles.shape
    return tiles.reshape(*shape[:dim], shape[dim] * shape[dim + 1], *shape[dim + 2 :])


def turned_blocks(tiles, axes, order):
    inside = tiles.shape[1:]
    out = tiles.reshape(*(lax.axis_size(a) for a in axes), *inside)
    for k in order:
        out = lax.all_to_all(out, axes[k], k, k, tiled=True)
    return out.reshape(-1, *inside)


def core_and_chips(value, groups, order, split_dim, concat_dim):
    length = lax.axis_size(groups[0]) * lax.axis_size(groups[1])
    tiles = in_blocks(value, split_dim, length)
    return in_order(turned_blocks(tiles, groups, order), concat_dim)


def coefficients(run_levels, class_ids):
    table = 0.03 * jnp.exp(run_levels.astype(jnp.float32) * jnp.log(jnp.float32(1.35)))
    kappa = jnp.zeros((run_levels.shape[0],) + class_ids.shape, jnp.float32)
    for klass in range(run_levels.shape[1]):
        picked = jnp.where(class_ids == klass, 1.0, 0.0).astype(jnp.float32)
        kappa = kappa + picked[None] * table[:, klass][:, None, None]
    return kappa


def advance(field, kappa, steep):
    ratio = field * field
    spread = kappa * (1.0 + steep * ratio) / (1.0 + ratio)
    fpad = jnp.pad(field, ((0, 0), (0, 0), (1, 1)))
    spad = jnp.pad(spread, ((0, 0), (0, 0), (1, 1)))
    centre = field[:, 1:-1]
    middle = spread[:, 1:-1]
    total = centre + 0.5 * (middle + spread[:, :-2]) * (field[:, :-2] - centre)
    total = total + 0.5 * (middle + spread[:, 2:]) * (field[:, 2:] - centre)
    total = total + 0.5 * (middle + spad[:, 1:-1, :-2]) * (fpad[:, 1:-1, :-2] - centre)
    total = total + 0.5 * (middle + spad[:, 1:-1, 2:]) * (fpad[:, 1:-1, 2:] - centre)
    return total


def features(run_levels, step_pick, steepness):
    count = run_levels.shape[0]
    onehot = (run_levels[:, :, None] == jnp.arange(LEVELS, dtype=jnp.int32)[None, None, :]).astype(
        jnp.float32
    )
    onehot = onehot.reshape(count, -1)
    moment = (step_pick[:, None] == jnp.arange(1, STEPS + 1, dtype=jnp.int32)[None, :]).astype(
        jnp.float32
    )
    return jnp.concatenate([onehot, moment, steepness[:, None]], axis=1)


def dsilu(pre):
    logistic = jax.nn.sigmoid(pre)
    return logistic * (1.0 + pre * (1.0 - logistic))


def on_device(
    start_field, class_ids, run_levels, steepness, step_pick, input_layer, output_layer, output_bias
):
    local_runs, rows, columns = start_field.shape
    first_run = lax.axis_index(GRP) * local_runs
    levels_here = lax.dynamic_slice_in_dim(run_levels, first_run, local_runs, 0)
    steep = lax.dynamic_slice_in_dim(steepness, first_run, local_runs, 0)[:, None, None]
    pick_here = lax.dynamic_slice_in_dim(step_pick, first_run, local_runs, 0)[:, None, None]
    snapshot = jnp.zeros_like(start_field)
    class_wide = with_halo(class_ids + 1, (("tile", 0),), STEPS)
    kappa_wide = coefficients(levels_here, class_wide - 1)
    wide = with_halo(start_field, (("tile", 1),), STEPS)
    first_row = lax.axis_index("tile") * rows - STEPS
    total_rows = rows * lax.axis_size("tile")
    span = kappa_wide.shape[1]
    for step in range(STEPS):
        margin = STEPS - step - 1
        kappa_now = kappa_wide[:, step : span - step]
        wide = advance(wide, kappa_now, steep)
        row_ids = first_row + step + 1 + jnp.arange(wide.shape[1], dtype=jnp.int32)
        inside = (row_ids >= 0) & (row_ids < total_rows)
        wide = jnp.where(inside[None, :, None], wide, 0.0)
        snapshot = jnp.where(pick_here == step + 1, wide[:, margin : margin + rows], snapshot)
    flat = snapshot.reshape(local_runs, rows * columns)
    target = core_and_chips(flat, ("grp_0", "grp_1"), (0, 1), 1, 0)
    runs_total = target.shape[0]
    feats = features(run_levels, step_pick, steepness)
    pre = jnp.dot(feats, input_layer, precision=lax.Precision.HIGHEST)
    hidden = jax.nn.silu(pre).astype(jnp.bfloat16)
    error = (
        jnp.dot(hidden, output_layer, preferred_element_type=jnp.float32)
        + output_bias[None, :]
        - target
    )
    slope = (error * (2.0 / runs_total)).astype(jnp.bfloat16)
    grad = lax.dot_general(
        hidden, slope, (((0,), (0,)), ((), ())), preferred_element_type=jnp.float32
    )
    output_next = (output_layer.astype(jnp.float32) - 0.5 * grad).astype(jnp.bfloat16)
    bias_next = output_bias - 0.5 * jnp.sum(slope.astype(jnp.float32), axis=0)
    gain_slope = dsilu(pre)
    partial_back = lax.dot_general(
        slope, output_layer, (((1,), (1,)), ((), ())), preferred_element_type=jnp.float32
    )
    back = lax.psum(partial_back, GRP_TILE)
    grad_in = lax.dot_general(
        feats, back * gain_slope, (((0,), (0,)), ((), ())), precision=lax.Precision.HIGHEST
    )
    input_next = input_layer - 2.0 * grad_in
    return (error.astype(jnp.bfloat16), output_next, bias_next, input_next)


def solution(mesh):
    split = Mesh(mesh.devices.reshape(2, 2, mesh.shape["tile"]), ("grp_0", "grp_1", "tile"))
    return jax.shard_map(
        on_device,
        mesh=split,
        in_specs=(
            P(GRP, "tile", None),
            P("tile", None),
            P(),
            P(),
            P(),
            P(),
            P(None, GRP_TILE),
            P(GRP_TILE),
        ),
        out_specs=(P(None, GRP_TILE), P(None, GRP_TILE), P(GRP_TILE), P()),
        check_vma=False,
    )
```

profile of v0, /device:TPU:1, one launch (start us, length us, event | category | flops | bytes accessed | tf_op | source)
XLA Modules:
  0.0 393.0 jit_solution(14505002223111617005)
XLA Ops:
  7.2 0.8 broadcast_add_fusion
  8.0 4.4 %collective-permute-start.2 = (s32[4,512]{1,0:T(4,128)S(1)}, s32[4,512]{1,0:T(4,128)S(1)}, u32[]{:S(2)}, u32[]{:S(2)}) collective-permute-start(s32[4,512]{1,0:T(4,128)S(1)} %get-tuple-element.24), channel_id=1, source_target_pairs={{0,1},{1,2},{2,3},{3,4},{4,5},{5,6},{6,7},{7,8},{8,9},{9,10},{10,1... | collective-permute-start | bytes 24584 | tf_op jit(solution)/shard_map/ppermute | solution.py:20
  12.3 1.3 collective-permute-start.3
  13.6 2.7 fusion.96
  16.4 0.3 copy.34
  16.7 4.2 %collective-permute-start = (f32[128,4,512]{2,0,1:T(8,128)S(1)}, f32[128,4,512]{2,0,1:T(8,128)S(1)}, u32[]{:S(2)}, u32[]{:S(2)}) collective-permute-start(f32[128,4,512]{2,0,1:T(8,128)S(1)} %copy.34), channel_id=1, source_target_pairs={{0,1},{1,2},{2,3},{3,4},{4,5},{5,6},{6,7},{7,8},{8,9},{9,10},{10,1... | collective-permute-start | bytes 3145736 | tf_op jit(solution)/shard_map/ppermute | solution.py:20
  21.0 1.3 copy.35
  22.3 1.3 collective-permute-start.1
  23.7 0.6 compare_and_fusion.3
  24.3 0.6 compare_and_fusion
  24.8 0.6 compare_and_fusion.1
  25.4 1.3 broadcast_compare_fusion.3
  26.7 0.6 broadcast_compare_fusion.2
  27.3 0.6 compare_and_fusion.2
  27.8 5.3 %copy.29 = f32[128,16,512]{0,2,1:T(8,128)} copy(f32[128,16,512]{2,1,0:T(8,128)} %param.8) | data formatting | bytes 8388608 | tf_op args[0]
  33.1 0.8 dynamic_slice.11
  34.0 14.8 %multiply_add_fusion = f32[128,24,512]{0,2,1:T(8,128)} fusion(f32[128]{0:T(128)S(1)} %get-tuple-element.27, f32[24,512]{1,0:T(8,128)S(1)} %get-tuple-element.23, f32[128]{0:T(128)S(1)} %get-tuple-element.28, f32[24,512]{1,0:T(8,128)S(1)} %get-tuple-element.22, f32[128]{0:T(128)S(1)} %get-tuple-element.29, f32[24,512]{1,0:T(8,128)S(1)} %get-tuple-element.21, ...), kind=kLoop, calls=%fused_computation.3 | loop fusion | flops 23592960 | bytes 6688768 | tf_op jit(solution)/shard_map/add | solution.py:57
  49.0 0.3 copy.28
  49.3 1.5 copy.30
  50.9 1.0 copy-done.3
  52.0 2.7 pad_maximum_fusion
  54.7 0.6 copy-done.2
  55.4 15.7 %add_divide_fusion = f32[128,24,512]{0,2,1:T(8,128)S(1)} fusion(f32[128]{0:T(128)S(1)} %dynamic_slice.11, f32[128,4,512]{0,2,1:T(8,128)} %copy-done.3, f32[128,16,512]{0,2,1:T(8,128)S(1)} %copy-done.2, f32[128,4,512]{0,2,1:T(8,128)S(1)} %copy.28, f32[128]{0:T(128)S(1)} %copy-done.25, f32[24,512]{1,0:T(8,128)S(1)} %copy-done.9, f32[128]{0:T(128)S(1)} %copy-done.27, ...), kind=kLoop, calls=%fused_computation.2 | loop fusion | flops 36175872 | bytes 12980736 | tf_op jit(solution)/shard_map/div | solution.py:63
  71.1 11.3 %fusion.11 = (f32[128,22,512]{0,2,1:T(8,128)}, f32[128,22,512]{0,2,1:T(8,128)S(1)}) fusion(f32[128,24,512]{0,2,1:T(8,128)} %multiply_add_fusion, f32[128]{0:T(128)S(1)} %dynamic_slice.11, f32[128,24,512]{0,2,1:T(8,128)S(1)} %pad_maximum_fusion, f32[128,24,512]{0,2,1:T(8,128)S(1)} %add_divide_fusion, pred[22]{0:T(512)(128)(4,1)} %compare_and_fusion), kind=kLoop, calls=%fused_computation.20 | loop fusion | flops 38928384 | bytes 64487960 | tf_op jit(solution)/shard_map/div | solution.py:63
  82.4 16.6 %fusion.29 = (f32[128,20,512]{0,2,1:T(8,128)S(1)}, f32[128,20,512]{0,2,1:T(8,128)S(1)}) fusion(f32[128,24,512]{0,2,1:T(8,128)} %multiply_add_fusion, f32[128]{0:T(128)S(1)} %dynamic_slice.11, f32[128,22,512]{0,2,1:T(8,128)S(1)} %get-tuple-element.11, f32[128,22,512]{0,2,1:T(8,128)} %get-tuple-element.10, pred[20]{0:T(512)(128)(4,1)S(1)} %copy-done.46), kind=kLoop, calls=%fused_computation.47 | loop fusion | flops 35389440 | bytes 58721280 | tf_op jit(solution)/shard_map/div | solution.py:63
  99.1 10.9 %fusion.47 = (f32[128,18,512]{0,2,1:T(8,128)}, f32[128,18,512]{0,2,1:T(8,128)}) fusion(f32[128,24,512]{0,2,1:T(8,128)} %multiply_add_fusion, f32[128]{0:T(128)S(1)} %dynamic_slice.11, f32[128,20,512]{0,2,1:T(8,128)S(1)} %get-tuple-element.9, f32[128,20,512]{0,2,1:T(8,128)S(1)} %get-tuple-element.8, pred[18]{0:T(512)(128)(4,1)S(1)} %copy-done.45), kind=kLoop, calls=%fused_computation.74 | loop fusion | flops 31850496 | bytes 52954112 | tf_op jit(solution)/shard_map/div | solution.py:63
  110.0 21.7 %fusion.60 = f32[128,16,512]{0,2,1:T(8,128)} fusion(f32[128,18,512]{0,2,1:T(8,128)} %get-tuple-element.6, f32[128,18,512]{0,2,1:T(8,128)} %get-tuple-element.7, f32[128,22,512]{0,2,1:T(8,128)} %copy-done, f32[128,20,512]{0,2,1:T(8,128)} %copy-done.1, pred[16]{0:T(512)(128)(4,1)S(1)} %copy-done.44, pred[128]{0:T(512)(128)(4,1)S(1)} %copy-done.43, ...), kind=kLoop, calls=%fused_computation.95 | loop fusion | flops 26214400 | bytes 47186448 | tf_op jit(solution)/shard_map/jit(_where)/select_n | solution.py:114
  131.7 5.6 %copy.31 = f32[4,128,2048]{2,1,0:T(8,128)} copy(f32[4,128,2048]{1,2,0:T(8,128)} %bitcast.30) | data formatting | bytes 8388608 | tf_op jit(solution)/shard_map/transpose | solution.py:29
  137.3 5.8 %all-to-all-start = ((f32[2,2,128,2048]{3,2,1,0:T(8,128)}), f32[2,2,128,2048]{3,2,1,0:T(8,128)}, u32[]{:S(2)}, u32[]{:S(2)}) async-start(f32[2,2,128,2048]{3,2,1,0:T(8,128)} %bitcast.31), calls=%async_computation | async-start | bytes 8388608 | tf_op jit(solution)/shard_map/all_to_all | solution.py:42
  143.0 0.0 all-reduce.10.cloned.1.call-start
  143.1 0.1 eq.141
  143.2 0.1 compare_convert_fusion
  143.3 0.1 fusion.87
  143.4 5.1 %fusion.88 = f32[512,2048]{1,0:T(8,128)} fusion(f32[69,2048]{1,0:T(8,128)S(1)} %copy-done.5, f32[512,1]{0,1:T(1,128)S(1)} %bitcast.32, f32[512,4]{0,1:T(4,128)S(1)} %compare_convert_fusion, f32[512,64]{0,1:T(8,128)S(1)} %fusion.87), kind=kOutput, calls=%fused_computation.131 | convolution fusion | flops 868291584 | bytes 4900864 | tf_op jit(solution)/shard_map/dot_general | solution.py:119
  148.5 42.2 %all-to-all-done = f32[2,2,128,2048]{3,2,1,0:T(8,128)} async-done(((f32[2,2,128,2048]{3,2,1,0:T(8,128)}), f32[2,2,128,2048]{3,2,1,0:T(8,128)}, u32[]{:S(2)}, u32[]{:S(2)}) %all-to-all-start) | async-done | bytes 4194336 | tf_op jit(solution)/shard_map/all_to_all | solution.py:42
  190.6 2.6 copy.32
  193.2 0.0 slice-start.1
  193.3 9.2 %all_to_all.10 = f32[2,2,128,2048]{3,2,0,1:T(8,128)S(1)} all-to-all(f32[2,2,128,2048]{3,2,0,1:T(8,128)S(1)} %copy.32), channel_id=1, replica_groups=mesh['grp_0'=2,'grp_1'=2,'tile'=32] {'grp_1'}, dimensions={1} | all-to-all | bytes 8388608 | tf_op jit(solution)/shard_map/all_to_all | solution.py:42
  202.5 0.5 copy.33
  203.0 1.7 copy-done.4
  204.7 6.1 %convert_reduce_fusion = (f32[2048]{0:T(1024)S(1)}, bf16[512,2048]{1,0:T(8,128)(2,1)}, f32[512,2048]{1,0:T(8,128)S(1)}) fusion(f32[2,2,128,2048]{3,2,1,0:T(8,128)S(1)} %copy.33, f32[2048]{0:T(1024)S(1)} %copy-done.23, bf16[2048,2048]{1,0:T(8,128)(2,1)S(1)} %bitcast.35, f32[512,2048]{1,0:T(8,128)S(1)} %copy-done.4), kind=kOutput, calls=%fused_computation.121 | convolution fusion | flops 4307548160 | bytes 23085056 | tf_op jit(solution)/shard_map/dot_general | solution.py:122
  210.7 2.1 copy-done.47
  212.8 6.2 %fusion.92 = f32[512,2048]{1,0:T(8,128)} fusion(bf16[2048,2048]{1,0:T(8,128)(2,1)S(1)} %bitcast.35, f32[512,2048]{1,0:T(8,128)S(1)} %get-tuple-element.37), kind=kOutput, calls=%fused_computation.165 | convolution fusion | flops 4297064448 | bytes 16777216 | tf_op jit(solution)/shard_map/dot_general | solution.py:133
  219.0 0.0 all-reduce.10.cloned.1.call-update
  219.0 0.6 multiply_subtract_fusion
  219.6 14.6 %subtract_convert_fusion = bf16[2048,2048]{1,0:T(8,128)(2,1)} fusion(bf16[2048,2048]{1,0:T(8,128)(2,1)} %param.14, f32[512,2048]{1,0:T(8,128)} %copy-done.47, f32[512,2048]{1,0:T(8,128)} %fusion.88), kind=kOutput, calls=%fused_computation | convolution fusion | flops 4319084544 | bytes 25165824 | tf_op jit(solution)/shard_map/dot_general | solution.py:127
  234.2 143.7 %all-reduce.10.cloned.1.call-done = f32[512,2048]{1,0:T(8,128)} async-done(((f32[512,2048]{1,0:T(8,128)}), f32[512,2048]{1,0:T(8,128)}) %all-reduce.10.cloned.1.call-update) | async-done | bytes 4194320 | tf_op jit(solution)/shard_map/psum | solution.py:136
  377.9 8.2 %fusion.83 = f32[69,2048]{1,0:T(8,128)} fusion(f32[69,2048]{1,0:T(8,128)S(1)} %copy-done.5, f32[512,2048]{1,0:T(8,128)} %all-reduce.10.cloned.1.call-done, f32[512,2048]{1,0:T(8,128)} %fusion.88, f32[512,1]{0,1:T(1,128)S(1)} %bitcast.33, f32[512,4]{0,1:T(4,128)S(1)} %compare_convert_fusion, f32[512,64]{0,1:T(8,128)S(1)} %fusion.87), kind=kOutput, calls=%fused_computation.126 | convolution fusion | flops 876962816 | bytes 9660416 | tf_op jit(solution)/shard_map/dot_general | solution.py:137
  (107 shorter events, 0.3 us)
Async XLA Ops:
  7.2 16.4 %copy-start.22 = (s32[512,8]{0,1:T(8,128)S(1)}, s32[512,8]{0,1:T(8,128)}, u32[]{:S(2)}) copy-start(s32[512,8]{0,1:T(8,128)} %param.10) | copy-start | bytes 49156
  8.0 25.9 %collective-permute-start.2 = (s32[4,512]{1,0:T(4,128)S(1)}, s32[4,512]{1,0:T(4,128)S(1)}, u32[]{:S(2)}, u32[]{:S(2)}) collective-permute-start(s32[4,512]{1,0:T(4,128)S(1)} %get-tuple-element.24), channel_id=1, source_target_pairs={{0,1},{1,2},{2,3},{3,4},{4,5},{5,6},{6,7},{7,8},{8,9},{9,10},{10,1... | collective-permute-start | bytes 24584 | tf_op jit(solution)/shard_map/ppermute | solution.py:20
  12.3 21.6 %collective-permute-start.3 = (s32[4,512]{1,0:T(4,128)S(1)}, s32[4,512]{1,0:T(4,128)S(1)}, u32[]{:S(2)}, u32[]{:S(2)}) collective-permute-start(s32[4,512]{1,0:T(4,128)S(1)} %get-tuple-element.25), channel_id=1, source_target_pairs={{1,0},{2,1},{3,2},{4,3},{5,4},{6,5},{7,6},{8,7},{9,8},{10,9},{11,1... | collective-permute-start | bytes 24584 | tf_op jit(solution)/shard_map/ppermute | solution.py:21
  16.7 32.2 %collective-permute-start = (f32[128,4,512]{2,0,1:T(8,128)S(1)}, f32[128,4,512]{2,0,1:T(8,128)S(1)}, u32[]{:S(2)}, u32[]{:S(2)}) collective-permute-start(f32[128,4,512]{2,0,1:T(8,128)S(1)} %copy.34), channel_id=1, source_target_pairs={{0,1},{1,2},{2,3},{3,4},{4,5},{5,6},{6,7},{7,8},{8,9},{9,10},{10,1... | collective-permute-start | bytes 3145736 | tf_op jit(solution)/shard_map/ppermute | solution.py:20
  22.3 27.0 %collective-permute-start.1 = (f32[128,4,512]{2,0,1:T(8,128)}, f32[128,4,512]{2,0,1:T(8,128)}, u32[]{:S(2)}, u32[]{:S(2)}) collective-permute-start(f32[128,4,512]{2,0,1:T(8,128)} %copy.35), channel_id=1, source_target_pairs={{1,0},{2,1},{3,2},{4,3},{5,4},{6,5},{7,6},{8,7},{9,8},{10,9},{11,1... | collective-permute-start | bytes 3145736 | tf_op jit(solution)/shard_map/ppermute | solution.py:21
  23.6 25.2 %copy-start.24 = (f32[128]{0:T(128)}, f32[128]{0:T(128)S(1)}, u32[]{:S(2)}) copy-start(f32[128]{0:T(128)S(1)} %get-tuple-element.27) | copy-start | bytes 1540
  23.6 25.2 %copy-start.26 = (f32[128]{0:T(128)}, f32[128]{0:T(128)S(1)}, u32[]{:S(2)}) copy-start(f32[128]{0:T(128)S(1)} %get-tuple-element.28) | copy-start | bytes 1540
  23.6 25.2 %copy-start.28 = (f32[128]{0:T(128)}, f32[128]{0:T(128)S(1)}, u32[]{:S(2)}) copy-start(f32[128]{0:T(128)S(1)} %get-tuple-element.29) | copy-start | bytes 1540
  23.6 25.2 %copy-start.30 = (f32[128]{0:T(128)}, f32[128]{0:T(128)S(1)}, u32[]{:S(2)}) copy-start(f32[128]{0:T(128)S(1)} %get-tuple-element.30) | copy-start | bytes 1540
  23.6 25.2 %copy-start.32 = (f32[128]{0:T(128)}, f32[128]{0:T(128)S(1)}, u32[]{:S(2)}) copy-start(f32[128]{0:T(128)S(1)} %get-tuple-element.31) | copy-start | bytes 1540
  23.7 25.2 %copy-start.34 = (f32[128]{0:T(128)}, f32[128]{0:T(128)S(1)}, u32[]{:S(2)}) copy-start(f32[128]{0:T(128)S(1)} %get-tuple-element.32) | copy-start | bytes 1540
  23.7 25.2 %copy-start.36 = (f32[128]{0:T(128)}, f32[128]{0:T(128)S(1)}, u32[]{:S(2)}) copy-start(f32[128]{0:T(128)S(1)} %get-tuple-element.33) | copy-start | bytes 1540
  33.9 15.0 %copy-start.6 = (f32[24,512]{1,0:T(8,128)}, f32[24,512]{1,0:T(8,128)S(1)}, u32[]{:S(2)}) copy-start(f32[24,512]{1,0:T(8,128)S(1)} %get-tuple-element.22) | copy-start | bytes 147460
  33.9 15.0 %copy-start.8 = (f32[24,512]{1,0:T(8,128)}, f32[24,512]{1,0:T(8,128)S(1)}, u32[]{:S(2)}) copy-start(f32[24,512]{1,0:T(8,128)S(1)} %get-tuple-element.23) | copy-start | bytes 147460
  34.0 14.9 %copy-start.10 = (f32[24,512]{1,0:T(8,128)}, f32[24,512]{1,0:T(8,128)S(1)}, u32[]{:S(2)}) copy-start(f32[24,512]{1,0:T(8,128)S(1)} %get-tuple-element.16) | copy-start | bytes 147460
  34.0 14.9 %copy-start.12 = (f32[24,512]{1,0:T(8,128)}, f32[24,512]{1,0:T(8,128)S(1)}, u32[]{:S(2)}) copy-start(f32[24,512]{1,0:T(8,128)S(1)} %get-tuple-element.17) | copy-start | bytes 147460
  34.0 14.9 %copy-start.14 = (f32[24,512]{1,0:T(8,128)}, f32[24,512]{1,0:T(8,128)S(1)}, u32[]{:S(2)}) copy-start(f32[24,512]{1,0:T(8,128)S(1)} %get-tuple-element.18) | copy-start | bytes 147460
  34.0 14.9 %copy-start.16 = (f32[24,512]{1,0:T(8,128)}, f32[24,512]{1,0:T(8,128)S(1)}, u32[]{:S(2)}) copy-start(f32[24,512]{1,0:T(8,128)S(1)} %get-tuple-element.19) | copy-start | bytes 147460
  34.0 14.9 %copy-start.18 = (f32[24,512]{1,0:T(8,128)}, f32[24,512]{1,0:T(8,128)S(1)}, u32[]{:S(2)}) copy-start(f32[24,512]{1,0:T(8,128)S(1)} %get-tuple-element.20) | copy-start | bytes 147460
  34.0 14.9 %copy-start.20 = (f32[24,512]{1,0:T(8,128)}, f32[24,512]{1,0:T(8,128)S(1)}, u32[]{:S(2)}) copy-start(f32[24,512]{1,0:T(8,128)S(1)} %get-tuple-element.21) | copy-start | bytes 147460
  51.9 3.4 copy-start.2
  51.9 3.4 copy-start.7
  51.9 3.5 copy-start.9
  51.9 3.5 copy-start.11
  51.9 3.4 copy-start.13
  51.9 3.4 copy-start.15
  51.9 3.4 copy-start.17
  51.9 3.4 copy-start.19
  51.9 3.4 copy-start.21
  51.9 3.4 copy-start.25
  51.9 3.4 copy-start.27
  51.9 3.4 copy-start.29
  71.1 11.3 %copy-start.46 = (pred[20]{0:T(512)(128)(4,1)S(1)}, pred[20]{0:T(512)(128)(4,1)}, u32[]{:S(2)}) copy-start(pred[20]{0:T(512)(128)(4,1)} %compare_and_fusion.1) | copy-start | bytes 64
  82.4 16.6 %copy-start = (f32[128,22,512]{0,2,1:T(8,128)}, f32[128,22,512]{0,2,1:T(8,128)S(1)}, u32[]{:S(2)}) copy-start(f32[128,22,512]{0,2,1:T(8,128)S(1)} %get-tuple-element.11) | copy-start | bytes 17301508
  82.4 16.7 %copy-start.45 = (pred[18]{0:T(512)(128)(4,1)S(1)}, pred[18]{0:T(512)(128)(4,1)}, u32[]{:S(2)}) copy-start(pred[18]{0:T(512)(128)(4,1)} %compare_and_fusion.2) | copy-start | bytes 58
  99.0 10.9 %copy-start.1 = (f32[128,20,512]{0,2,1:T(8,128)}, f32[128,20,512]{0,2,1:T(8,128)S(1)}, u32[]{:S(2)}) copy-start(f32[128,20,512]{0,2,1:T(8,128)S(1)} %get-tuple-element.9) | copy-start | bytes 15728644
  99.0 10.9 %copy-start.40 = (pred[128]{0:T(512)(128)(4,1)S(1)}, pred[128]{0:T(512)(128)(4,1)}, u32[]{:S(2)}) copy-start(pred[128]{0:T(512)(128)(4,1)} %get-tuple-element.4) | copy-start | bytes 388
  99.0 10.9 %copy-start.41 = (pred[128]{0:T(512)(128)(4,1)S(1)}, pred[128]{0:T(512)(128)(4,1)}, u32[]{:S(2)}) copy-start(pred[128]{0:T(512)(128)(4,1)} %get-tuple-element.34) | copy-start | bytes 388
  99.0 10.9 %copy-start.42 = (pred[128]{0:T(512)(128)(4,1)S(1)}, pred[128]{0:T(512)(128)(4,1)}, u32[]{:S(2)}) copy-start(pred[128]{0:T(512)(128)(4,1)} %get-tuple-element.35) | copy-start | bytes 388
  99.1 10.9 %copy-start.43 = (pred[128]{0:T(512)(128)(4,1)S(1)}, pred[128]{0:T(512)(128)(4,1)}, u32[]{:S(2)}) copy-start(pred[128]{0:T(512)(128)(4,1)} %get-tuple-element.36) | copy-start | bytes 388
  99.1 10.9 %copy-start.44 = (pred[16]{0:T(512)(128)(4,1)S(1)}, pred[16]{0:T(512)(128)(4,1)}, u32[]{:S(2)}) copy-start(pred[16]{0:T(512)(128)(4,1)} %compare_and_fusion.3) | copy-start | bytes 52
  137.3 5.9 %copy-start.38 = (s32[512]{0:T(512)S(1)}, s32[512]{0:T(512)}, u32[]{:S(2)}) copy-start(s32[512]{0:T(512)} %param.12) | copy-start | bytes 6148
  137.3 6.1 %copy-start.5 = (f32[69,2048]{1,0:T(8,128)S(1)}, f32[69,2048]{1,0:T(8,128)}, u32[]{:S(2)}) copy-start(f32[69,2048]{1,0:T(8,128)} %param.13) | copy-start | bytes 1695748
  137.3 6.1 %copy-start.39 = (f32[512]{0:T(512)S(1)}, f32[512]{0:T(512)}, u32[]{:S(2)}) copy-start(f32[512]{0:T(512)} %param.11) | copy-start | bytes 6148
  137.3 53.4 %all-to-all-start = ((f32[2,2,128,2048]{3,2,1,0:T(8,128)}), f32[2,2,128,2048]{3,2,1,0:T(8,128)}, u32[]{:S(2)}, u32[]{:S(2)}) async-start(f32[2,2,128,2048]{3,2,1,0:T(8,128)} %bitcast.31), calls=%async_computation | async-start | bytes 8388608 | tf_op jit(solution)/shard_map/all_to_all | solution.py:42
  143.0 234.9 %all-reduce.10.cloned.1.call-start = ((), (), s32[]{:S(2)}) async-start(), calls=%async_computation.2 | async-start | bytes 8388608 | tf_op jit(solution)/shard_map/psum | solution.py:136
  190.6 12.4 %slice-start = ((s8[8388608]{0:T(1024)(128)(4,1)}), s8[4194304]{0:T(1024)(128)(4,1)S(1)}, s32[]{:S(2)}) async-start(s8[8388608]{0:T(1024)(128)(4,1)} %bitcast.34), calls=%async_computation.3 | async-start | bytes 8388608
  193.2 9.8 %slice-start.1 = ((s8[8388608]{0:T(1024)(128)(4,1)}), s8[4194304]{0:T(1024)(128)(4,1)S(1)}, s32[]{:S(2)}) async-start(s8[8388608]{0:T(1024)(128)(4,1)} %bitcast.34), calls=%async_computation.4 | async-start | bytes 8388608
  (8 other events, 21.2 us)
Sparse Core Ops, SparseCore 0:
  219.1 158.7 all-reduce.9
where the time goes:
time: 394 us; the launch traced here: 393 us
  waiting for transfers between devices  186 us (47%)
  other arithmetic  99.4 us (25%)
  matrix products  40.2 us (10%)
  local copies, waits for them, and re-layouts  26.5 us (7%)
  starting transfers between devices  17 us (4%)
  between operations  14.8 us (4%)
  blocking collectives  9.24 us (2%)
    psum x1, waiting for transfers between devices, on_device(): back = lax.psum(partial_back, GRP_TILE)  144 us
    div x4, other arithmetic, advance(): spread = kappa * (1.0 + steep * ratio) / (1.0 + ratio)  54.4 us
    all_to_all x1, waiting for transfers between devices, turned_blocks(): out = lax.all_to_all(out, axes[k], k, k, tiled=True)  42.2 us
    select_n x1, other arithmetic, on_device(): jnp.where(pick_here == step + 1, wide[:, margin:margin + rows], snapshot)  21.7 us
    add x1, other arithmetic, coefficients(): kappa = kappa + picked[None] * table[:, klass][:, None, None]  14.8 us
    dot_general x1, matrix products, on_device(): lax.dot_general(hidden, slope, (((0,), (0,)), ((), ())), preferred_elemen...  14.6 us
    unnamed x103, local copies, waits for them, and re-layouts  12.4 us
    all_to_all x1, blocking collectives, turned_blocks(): out = lax.all_to_all(out, axes[k], k, k, tiled=True)  9.24 us
  transfers between devices with their start and end apart: 6, of which 2 were waited for; matrix products, arithmetic and copies ran while one was open for 13% of the time, Pallas kernels for 0%

commit v1 on v0

--- a/solution.py
+++ b/solution.py
@@ -133,7 +133,7 @@
     partial_back = lax.dot_general(
         slope, output_layer, (((1,), (1,)), ((), ())), preferred_element_type=jnp.float32
     )
-    back = lax.psum(partial_back, GRP_TILE)
+    back = jax.lax.psum(jax.lax.psum(partial_back, axis_name="grp_0"), axis_name=("grp_1", "tile"))
     grad_in = lax.dot_general(
         feats, back * gain_slope, (((0,), (0,)), ((), ())), precision=lax.Precision.HIGHEST
     )

time: 394 us -> 969 us (2.46); the launches traced: 393 us -> 952 us
  waiting for transfers between devices: 186 us -> 745 us
    psum x1 -> x2, waiting for transfers between devices: 144 us -> 702 us  [the longest x1 582 us: on_device(): jax.lax.psum(jax.lax.psum(partial_back, axis_name='grp_0'), axis_name=('g...]
  transfers between devices with their start and end apart: 6 -> 7, of which waited for: 2 -> 3; matrix products, arithmetic and copies ran while one was open for 13% -> 5% of each run, Pallas kernels for 0% -> 0%
where the time goes in v1:
time: 969 us; the launch traced here: 952 us
  waiting for transfers between devices  745 us (77%)
  other arithmetic  99.4 us (10%)
  matrix products  40.1 us (4%)
  local copies, waits for them, and re-layouts  26.4 us (3%)
  starting transfers between devices  17.3 us (2%)
  between operations  14.8 us (2%)
    psum x1, waiting for transfers between devices, on_device(): jax.lax.psum(jax.lax.psum(partial_back, axis_name='grp_0'), axis_name=('g...  582 us
    psum x1, waiting for transfers between devices, on_device(): jax.lax.psum(partial_back, axis_name='grp_0')  120 us
    div x4, other arithmetic, advance(): spread = kappa * (1.0 + steep * ratio) / (1.0 + ratio)  54.4 us
    all_to_all x1, waiting for transfers between devices, turned_blocks(): out = lax.all_to_all(out, axes[k], k, k, tiled=True)  42.2 us
    select_n x1, other arithmetic, on_device(): jnp.where(pick_here == step + 1, wide[:, margin:margin + rows], snapshot)  21.7 us
  transfers between devices with their start and end apart: 7, of which 3 were waited for; matrix products, arithmetic and copies ran while one was open for 5% of the time, Pallas kernels for 0%

profile of v1, /device:TPU:1, one launch (start us, length us, event | category | flops | bytes accessed | tf_op | source)
XLA Modules:
  0.0 951.9 jit_solution(806825170667194145)
XLA Ops:
  7.2 0.8 broadcast_add_fusion
  8.0 4.4 collective-permute-start.2
  12.3 1.3 collective-permute-start.3
  13.6 2.7 fusion.96
  16.4 0.3 copy.34
  16.7 4.2 collective-permute-start
  21.0 1.3 copy.35
  22.3 1.3 collective-permute-start.1
  23.7 0.6 compare_and_fusion.3
  24.3 0.6 compare_and_fusion
  24.8 0.6 compare_and_fusion.1
  25.4 1.3 broadcast_compare_fusion.3
  26.7 0.6 broadcast_compare_fusion.2
  27.3 0.6 compare_and_fusion.2
  27.8 5.3 copy.29
  33.1 0.8 dynamic_slice.11
  34.0 14.8 %multiply_add_fusion = f32[128,24,512]{0,2,1:T(8,128)} fusion(f32[128]{0:T(128)S(1)} %get-tuple-element.27, f32[24,512]{1,0:T(8,128)S(1)} %get-tuple-element.23, f32[128]{0:T(128)S(1)} %get-tuple-element.28, f32[24,512]{1,0:T(8,128)S(1)} %get-tuple-element.22, f32[128]{0:T(128)S(1)} %get-tuple-element.29, f32[24,512]{1,0:T(8,128)S(1)} %get-tuple-element.21, ...), kind=kLoop, calls=%fused_computation.3 | loop fusion | flops 23592960 | bytes 6688768 | tf_op jit(solution)/shard_map/add | solution.py:57
  49.0 0.3 copy.28
  49.3 1.5 copy.30
  50.9 1.0 copy-done.3
  52.0 2.7 pad_maximum_fusion
  54.7 0.6 copy-done.2
  55.4 15.7 %add_divide_fusion = f32[128,24,512]{0,2,1:T(8,128)S(1)} fusion(f32[128]{0:T(128)S(1)} %dynamic_slice.11, f32[128,4,512]{0,2,1:T(8,128)} %copy-done.3, f32[128,16,512]{0,2,1:T(8,128)S(1)} %copy-done.2, f32[128,4,512]{0,2,1:T(8,128)S(1)} %copy.28, f32[128]{0:T(128)S(1)} %copy-done.25, f32[24,512]{1,0:T(8,128)S(1)} %copy-done.9, f32[128]{0:T(128)S(1)} %copy-done.27, ...), kind=kLoop, calls=%fused_computation.2 | loop fusion | flops 36175872 | bytes 12980736 | tf_op jit(solution)/shard_map/div | solution.py:63
  71.1 11.3 %fusion.11 = (f32[128,22,512]{0,2,1:T(8,128)}, f32[128,22,512]{0,2,1:T(8,128)S(1)}) fusion(f32[128,24,512]{0,2,1:T(8,128)} %multiply_add_fusion, f32[128]{0:T(128)S(1)} %dynamic_slice.11, f32[128,24,512]{0,2,1:T(8,128)S(1)} %pad_maximum_fusion, f32[128,24,512]{0,2,1:T(8,128)S(1)} %add_divide_fusion, pred[22]{0:T(512)(128)(4,1)} %compare_and_fusion), kind=kLoop, calls=%fused_computation.20 | loop fusion | flops 38928384 | bytes 64487960 | tf_op jit(solution)/shard_map/div | solution.py:63
  82.4 16.6 %fusion.29 = (f32[128,20,512]{0,2,1:T(8,128)S(1)}, f32[128,20,512]{0,2,1:T(8,128)S(1)}) fusion(f32[128,24,512]{0,2,1:T(8,128)} %multiply_add_fusion, f32[128]{0:T(128)S(1)} %dynamic_slice.11, f32[128,22,512]{0,2,1:T(8,128)S(1)} %get-tuple-element.11, f32[128,22,512]{0,2,1:T(8,128)} %get-tuple-element.10, pred[20]{0:T(512)(128)(4,1)S(1)} %copy-done.46), kind=kLoop, calls=%fused_computation.47 | loop fusion | flops 35389440 | bytes 58721280 | tf_op jit(solution)/shard_map/div | solution.py:63
  99.1 10.9 %fusion.47 = (f32[128,18,512]{0,2,1:T(8,128)}, f32[128,18,512]{0,2,1:T(8,128)}) fusion(f32[128,24,512]{0,2,1:T(8,128)} %multiply_add_fusion, f32[128]{0:T(128)S(1)} %dynamic_slice.11, f32[128,20,512]{0,2,1:T(8,128)S(1)} %get-tuple-element.9, f32[128,20,512]{0,2,1:T(8,128)S(1)} %get-tuple-element.8, pred[18]{0:T(512)(128)(4,1)S(1)} %copy-done.45), kind=kLoop, calls=%fused_computation.74 | loop fusion | flops 31850496 | bytes 52954112 | tf_op jit(solution)/shard_map/div | solution.py:63
  110.0 21.7 %fusion.60 = f32[128,16,512]{0,2,1:T(8,128)} fusion(f32[128,18,512]{0,2,1:T(8,128)} %get-tuple-element.6, f32[128,18,512]{0,2,1:T(8,128)} %get-tuple-element.7, f32[128,22,512]{0,2,1:T(8,128)} %copy-done, f32[128,20,512]{0,2,1:T(8,128)} %copy-done.1, pred[16]{0:T(512)(128)(4,1)S(1)} %copy-done.44, pred[128]{0:T(512)(128)(4,1)S(1)} %copy-done.43, ...), kind=kLoop, calls=%fused_computation.95 | loop fusion | flops 26214400 | bytes 47186448 | tf_op jit(solution)/shard_map/jit(_where)/select_n | solution.py:114
  131.7 5.6 copy.31
  137.3 5.8 all-to-all-start
  143.0 0.0 all-reduce.11.cloned.1.call-start
  143.1 0.1 eq.141
  143.2 0.1 compare_convert_fusion
  143.3 0.1 fusion.87
  143.4 5.1 fusion.88
  148.5 42.2 %all-to-all-done = f32[2,2,128,2048]{3,2,1,0:T(8,128)} async-done(((f32[2,2,128,2048]{3,2,1,0:T(8,128)}), f32[2,2,128,2048]{3,2,1,0:T(8,128)}, u32[]{:S(2)}, u32[]{:S(2)}) %all-to-all-start) | async-done | bytes 4194336 | tf_op jit(solution)/shard_map/all_to_all | solution.py:42
  190.6 2.6 copy.32
  193.3 9.2 all_to_all.10
  202.5 0.5 copy.33
  203.0 1.7 copy-done.4
  204.7 6.1 convert_reduce_fusion
  210.7 1.9 copy-done.47
  212.7 6.1 fusion.92
  218.8 0.3 all-reduce.13.cloned.1.call-start
  219.1 120.4 %all-reduce.11.cloned.1.call-done = f32[512,2048]{1,0:T(8,128)} async-done(((f32[512,2048]{1,0:T(8,128)}), f32[512,2048]{1,0:T(8,128)}) %all-reduce.11.cloned.1.call-update) | async-done | bytes 4194320 | tf_op jit(solution)/shard_map/psum | solution.py:136
  339.5 0.6 multiply_subtract_fusion
  340.1 14.6 %subtract_convert_fusion = bf16[2048,2048]{1,0:T(8,128)(2,1)} fusion(bf16[2048,2048]{1,0:T(8,128)(2,1)} %param.14, f32[512,2048]{1,0:T(8,128)} %copy-done.47, f32[512,2048]{1,0:T(8,128)} %fusion.88), kind=kOutput, calls=%fused_computation | convolution fusion | flops 4319084544 | bytes 25165824 | tf_op jit(solution)/shard_map/dot_general | solution.py:127
  354.7 582.1 %all-reduce.13.cloned.1.call-done = f32[512,2048]{1,0:T(8,128)} async-done(((f32[512,2048]{1,0:T(8,128)}), f32[512,2048]{1,0:T(8,128)}) %all-reduce.13.cloned.1.call-update) | async-done | bytes 4194320 | tf_op jit(solution)/shard_map/psum | solution.py:136
  936.8 8.2 fusion.83
  (110 shorter events, 0.3 us)
Async XLA Ops:
  7.2 16.4 %copy-start.22 = (s32[512,8]{0,1:T(8,128)S(1)}, s32[512,8]{0,1:T(8,128)}, u32[]{:S(2)}) copy-start(s32[512,8]{0,1:T(8,128)} %param.10) | copy-start | bytes 49156
  8.0 25.9 %collective-permute-start.2 = (s32[4,512]{1,0:T(4,128)S(1)}, s32[4,512]{1,0:T(4,128)S(1)}, u32[]{:S(2)}, u32[]{:S(2)}) collective-permute-start(s32[4,512]{1,0:T(4,128)S(1)} %get-tuple-element.24), channel_id=1, source_target_pairs={{0,1},{1,2},{2,3},{3,4},{4,5},{5,6},{6,7},{7,8},{8,9},{9,10},{10,1... | collective-permute-start | bytes 24584 | tf_op jit(solution)/shard_map/ppermute | solution.py:20
  12.3 21.6 %collective-permute-start.3 = (s32[4,512]{1,0:T(4,128)S(1)}, s32[4,512]{1,0:T(4,128)S(1)}, u32[]{:S(2)}, u32[]{:S(2)}) collective-permute-start(s32[4,512]{1,0:T(4,128)S(1)} %get-tuple-element.25), channel_id=1, source_target_pairs={{1,0},{2,1},{3,2},{4,3},{5,4},{6,5},{7,6},{8,7},{9,8},{10,9},{11,1... | collective-permute-start | bytes 24584 | tf_op jit(solution)/shard_map/ppermute | solution.py:21
  16.7 32.2 %collective-permute-start = (f32[128,4,512]{2,0,1:T(8,128)S(1)}, f32[128,4,512]{2,0,1:T(8,128)S(1)}, u32[]{:S(2)}, u32[]{:S(2)}) collective-permute-start(f32[128,4,512]{2,0,1:T(8,128)S(1)} %copy.34), channel_id=1, source_target_pairs={{0,1},{1,2},{2,3},{3,4},{4,5},{5,6},{6,7},{7,8},{8,9},{9,10},{10,1... | collective-permute-start | bytes 3145736 | tf_op jit(solution)/shard_map/ppermute | solution.py:20
  22.3 27.0 %collective-permute-start.1 = (f32[128,4,512]{2,0,1:T(8,128)}, f32[128,4,512]{2,0,1:T(8,128)}, u32[]{:S(2)}, u32[]{:S(2)}) collective-permute-start(f32[128,4,512]{2,0,1:T(8,128)} %copy.35), channel_id=1, source_target_pairs={{1,0},{2,1},{3,2},{4,3},{5,4},{6,5},{7,6},{8,7},{9,8},{10,9},{11,1... | collective-permute-start | bytes 3145736 | tf_op jit(solution)/shard_map/ppermute | solution.py:21
  23.6 25.2 %copy-start.24 = (f32[128]{0:T(128)}, f32[128]{0:T(128)S(1)}, u32[]{:S(2)}) copy-start(f32[128]{0:T(128)S(1)} %get-tuple-element.27) | copy-start | bytes 1540
  23.6 25.2 %copy-start.26 = (f32[128]{0:T(128)}, f32[128]{0:T(128)S(1)}, u32[]{:S(2)}) copy-start(f32[128]{0:T(128)S(1)} %get-tuple-element.28) | copy-start | bytes 1540
  23.6 25.2 %copy-start.28 = (f32[128]{0:T(128)}, f32[128]{0:T(128)S(1)}, u32[]{:S(2)}) copy-start(f32[128]{0:T(128)S(1)} %get-tuple-element.29) | copy-start | bytes 1540
  23.6 25.2 %copy-start.30 = (f32[128]{0:T(128)}, f32[128]{0:T(128)S(1)}, u32[]{:S(2)}) copy-start(f32[128]{0:T(128)S(1)} %get-tuple-element.30) | copy-start | bytes 1540
  23.6 25.2 %copy-start.32 = (f32[128]{0:T(128)}, f32[128]{0:T(128)S(1)}, u32[]{:S(2)}) copy-start(f32[128]{0:T(128)S(1)} %get-tuple-element.31) | copy-start | bytes 1540
  23.7 25.2 %copy-start.34 = (f32[128]{0:T(128)}, f32[128]{0:T(128)S(1)}, u32[]{:S(2)}) copy-start(f32[128]{0:T(128)S(1)} %get-tuple-element.32) | copy-start | bytes 1540
  23.7 25.2 %copy-start.36 = (f32[128]{0:T(128)}, f32[128]{0:T(128)S(1)}, u32[]{:S(2)}) copy-start(f32[128]{0:T(128)S(1)} %get-tuple-element.33) | copy-start | bytes 1540
  33.9 15.0 %copy-start.6 = (f32[24,512]{1,0:T(8,128)}, f32[24,512]{1,0:T(8,128)S(1)}, u32[]{:S(2)}) copy-start(f32[24,512]{1,0:T(8,128)S(1)} %get-tuple-element.22) | copy-start | bytes 147460
  33.9 15.0 %copy-start.8 = (f32[24,512]{1,0:T(8,128)}, f32[24,512]{1,0:T(8,128)S(1)}, u32[]{:S(2)}) copy-start(f32[24,512]{1,0:T(8,128)S(1)} %get-tuple-element.23) | copy-start | bytes 147460
  34.0 14.9 %copy-start.10 = (f32[24,512]{1,0:T(8,128)}, f32[24,512]{1,0:T(8,128)S(1)}, u32[]{:S(2)}) copy-start(f32[24,512]{1,0:T(8,128)S(1)} %get-tuple-element.16) | copy-start | bytes 147460
  34.0 14.9 %copy-start.12 = (f32[24,512]{1,0:T(8,128)}, f32[24,512]{1,0:T(8,128)S(1)}, u32[]{:S(2)}) copy-start(f32[24,512]{1,0:T(8,128)S(1)} %get-tuple-element.17) | copy-start | bytes 147460
  34.0 14.9 %copy-start.14 = (f32[24,512]{1,0:T(8,128)}, f32[24,512]{1,0:T(8,128)S(1)}, u32[]{:S(2)}) copy-start(f32[24,512]{1,0:T(8,128)S(1)} %get-tuple-element.18) | copy-start | bytes 147460
  34.0 14.9 %copy-start.16 = (f32[24,512]{1,0:T(8,128)}, f32[24,512]{1,0:T(8,128)S(1)}, u32[]{:S(2)}) copy-start(f32[24,512]{1,0:T(8,128)S(1)} %get-tuple-element.19) | copy-start | bytes 147460
  34.0 14.9 %copy-start.18 = (f32[24,512]{1,0:T(8,128)}, f32[24,512]{1,0:T(8,128)S(1)}, u32[]{:S(2)}) copy-start(f32[24,512]{1,0:T(8,128)S(1)} %get-tuple-element.20) | copy-start | bytes 147460
  34.0 14.9 %copy-start.20 = (f32[24,512]{1,0:T(8,128)}, f32[24,512]{1,0:T(8,128)S(1)}, u32[]{:S(2)}) copy-start(f32[24,512]{1,0:T(8,128)S(1)} %get-tuple-element.21) | copy-start | bytes 147460
  51.9 3.4 copy-start.2
  51.9 3.4 copy-start.7
  51.9 3.5 copy-start.9
  51.9 3.5 copy-start.11
  51.9 3.4 copy-start.13
  51.9 3.4 copy-start.15
  51.9 3.4 copy-start.17
  51.9 3.4 copy-start.19
  51.9 3.4 copy-start.21
  51.9 3.4 copy-start.25
  51.9 3.4 copy-start.27
  71.1 11.3 %copy-start.46 = (pred[20]{0:T(512)(128)(4,1)S(1)}, pred[20]{0:T(512)(128)(4,1)}, u32[]{:S(2)}) copy-start(pred[20]{0:T(512)(128)(4,1)} %compare_and_fusion.1) | copy-start | bytes 64
  82.4 16.6 %copy-start = (f32[128,22,512]{0,2,1:T(8,128)}, f32[128,22,512]{0,2,1:T(8,128)S(1)}, u32[]{:S(2)}) copy-start(f32[128,22,512]{0,2,1:T(8,128)S(1)} %get-tuple-element.11) | copy-start | bytes 17301508
  82.4 16.7 %copy-start.45 = (pred[18]{0:T(512)(128)(4,1)S(1)}, pred[18]{0:T(512)(128)(4,1)}, u32[]{:S(2)}) copy-start(pred[18]{0:T(512)(128)(4,1)} %compare_and_fusion.2) | copy-start | bytes 58
  99.0 10.9 %copy-start.1 = (f32[128,20,512]{0,2,1:T(8,128)}, f32[128,20,512]{0,2,1:T(8,128)S(1)}, u32[]{:S(2)}) copy-start(f32[128,20,512]{0,2,1:T(8,128)S(1)} %get-tuple-element.9) | copy-start | bytes 15728644
  99.0 10.9 %copy-start.40 = (pred[128]{0:T(512)(128)(4,1)S(1)}, pred[128]{0:T(512)(128)(4,1)}, u32[]{:S(2)}) copy-start(pred[128]{0:T(512)(128)(4,1)} %get-tuple-element.4) | copy-start | bytes 388
  99.0 10.9 %copy-start.41 = (pred[128]{0:T(512)(128)(4,1)S(1)}, pred[128]{0:T(512)(128)(4,1)}, u32[]{:S(2)}) copy-start(pred[128]{0:T(512)(128)(4,1)} %get-tuple-element.34) | copy-start | bytes 388
  99.0 10.9 %copy-start.42 = (pred[128]{0:T(512)(128)(4,1)S(1)}, pred[128]{0:T(512)(128)(4,1)}, u32[]{:S(2)}) copy-start(pred[128]{0:T(512)(128)(4,1)} %get-tuple-element.35) | copy-start | bytes 388
  99.1 10.9 %copy-start.43 = (pred[128]{0:T(512)(128)(4,1)S(1)}, pred[128]{0:T(512)(128)(4,1)}, u32[]{:S(2)}) copy-start(pred[128]{0:T(512)(128)(4,1)} %get-tuple-element.36) | copy-start | bytes 388
  99.1 10.9 %copy-start.44 = (pred[16]{0:T(512)(128)(4,1)S(1)}, pred[16]{0:T(512)(128)(4,1)}, u32[]{:S(2)}) copy-start(pred[16]{0:T(512)(128)(4,1)} %compare_and_fusion.3) | copy-start | bytes 52
  137.3 5.9 copy-start.38
  137.3 6.1 copy-start.5
  137.3 6.1 copy-start.39
  137.3 53.4 %all-to-all-start = ((f32[2,2,128,2048]{3,2,1,0:T(8,128)}), f32[2,2,128,2048]{3,2,1,0:T(8,128)}, u32[]{:S(2)}, u32[]{:S(2)}) async-start(f32[2,2,128,2048]{3,2,1,0:T(8,128)} %bitcast.31), calls=%async_computation | async-start | bytes 8388608 | tf_op jit(solution)/shard_map/all_to_all | solution.py:42
  143.0 196.4 %all-reduce.11.cloned.1.call-start = ((), (), s32[]{:S(2)}) async-start(), calls=%async_computation.2 | async-start | bytes 8388608 | tf_op jit(solution)/shard_map/psum | solution.py:136
  190.6 12.4 %slice-start = ((s8[8388608]{0:T(1024)(128)(4,1)}), s8[4194304]{0:T(1024)(128)(4,1)S(1)}, s32[]{:S(2)}) async-start(s8[8388608]{0:T(1024)(128)(4,1)} %bitcast.34), calls=%async_computation.4 | async-start | bytes 8388608
  193.2 9.8 %slice-start.1 = ((s8[8388608]{0:T(1024)(128)(4,1)}), s8[4194304]{0:T(1024)(128)(4,1)S(1)}, s32[]{:S(2)}) async-start(s8[8388608]{0:T(1024)(128)(4,1)} %bitcast.34), calls=%async_computation.5 | async-start | bytes 8388608
  218.8 718.0 %all-reduce.13.cloned.1.call-start = ((), (), s32[]{:S(2)}) async-start(), calls=%async_computation.3 | async-start | bytes 8388608 | tf_op jit(solution)/shard_map/psum | solution.py:136
  (9 other events, 24.5 us)
Sparse Core Ops, SparseCore 0:
  218.9 120.4 all-reduce.10
  342.1 594.6 all-reduce.12
